TPU v7x, 128 devices: a whole 4x4x4 slice. The times are simulated.
128 devices in a mesh: gx: 4 (over z_lo, core), gy: 8 (over y, z_hi), gz: 4 (over x).
Axes of the slice: x: 4, y: 4, z: 4 (z_hi: 2, z_lo: 2; z = z_hi * 2 + z_lo), core: 2. Of those that a mesh axis runs over, the one named last changes fastest.
Arguments:
- saved: float32 [3, 27, 32, 64, 512], P(None, None, 'gx', 'gy', 'gz'), may hold values from 0.02 to 0.08
- porosity: float32 [32, 64, 512], P('gx', 'gy', 'gz'), may hold values from 0.05 to 0.6
- fluid: int32 [32, 64, 512], P('gx', 'gy', 'gz'), may hold values 0 or 1
- seed_adjoint: float32 [27, 32, 64, 512], P(None, 'gx', 'gy', 'gz'), may hold values from -6 to 6
Outputs:
- adjoint_first: float32 [27, 32, 64, 512], P(None, 'gx', 'gy', 'gz')
- porosity_grad: float32 [32, 64, 512], P('gx', 'gy', 'gz')
All inputs are finite; a program needn't handle non-finite values. No bound on the sum of `fluid` on one device may be relied on, other than what follows from the above.
Results may differ from a plain program's by a relative error of at most 0.0001.
Values sent between devices are 32-bit elements; how exact they have to be, the bound alone decides.
A program may use at most 64 MiB of HBM per device.

v0:
```python
import functools
import itertools

import jax
import jax.numpy as jnp
from jax import lax
from jax.experimental import pallas as pl
from jax.experimental.pallas import tpu as pltpu
from jax.sharding import PartitionSpec as P

STEPS = 3
AXES = ("gx", "gy", "gz")
OFFSETS = sorted(
    (o for o in itertools.product((-1, 0, 1), repeat=3) if any(o)),
    key=lambda o: (o[2] != 0, sum(map(abs, o)), o[0] != 0),
)
PAIRS = tuple(itertools.product(range(3), range(3)))


def f_moments(pops):
    s = [[pops(a, b, 0) + pops(a, b, 1) + pops(a, b, 2) for b in range(3)] for a in range(3)]
    dz = [sum(pops(a, b, 2) - pops(a, b, 0) for b in range(3)) for a in range(3)]
    sy = [s[a][0] + s[a][1] + s[a][2] for a in range(3)]
    dy = [s[a][2] - s[a][0] for a in range(3)]
    return (
        sy[0] + sy[1] + sy[2],
        sy[2] - sy[0],
        dy[0] + dy[1] + dy[2],
        dz[0] + dz[1] + dz[2],
    )


def even(v):
    side = v[0] + v[2]
    return 4.0 * v[1] + side, v[2] - v[0], side


def weighted_moments(p):
    z = [[even([p[a][b][c] for c in range(3)]) for b in range(3)] for a in range(3)]
    y = []
    for a in range(3):
        z0, z1, z2 = ([z[a][b][k] for b in range(3)] for k in range(3))
        y00, y10, y20 = even(z0)
        y01, y11, _ = even(z1)
        y02, _, _ = even(z2)
        y.append((y00, y10, y20, y01, y11, y02))
    p0, px, pxx = even([y[a][0] for a in range(3)])
    py, pxy, _ = even([y[a][1] for a in range(3)])
    pyy, _, _ = even([y[a][2] for a in range(3)])
    pz, pxz, _ = even([y[a][3] for a in range(3)])
    pyz, _, _ = even([y[a][4] for a in range(3)])
    pzz, _, _ = even([y[a][5] for a in range(3)])
    return p0, (px, py, pz), (pxx, pyy, pzz, pxy, pxz, pyz)


def kernel(
    sizes, saved, poro, fluid, seed, out, grad,
    adj, pops, flow, por, flu, res, acc, ztile, zrecv,
    lsem, osem, ssem, rsem,
):
    me = [lax.axis_index(a) for a in AXES]

    def exists(off):
        found = None
        for i, o in enumerate(off):
            if o:
                here = me[i] < sizes[i] - 1 if o > 0 else me[i] > 0
                found = here if found is None else jnp.logical_and(found, here)
        return found

    def device(off):
        return tuple(m + o for m, o in zip(me, off))

    def back(off):
        return tuple(-o for o in off)

    loads = [pltpu.make_async_copy(seed, adj.at[0, :, :, :, pl.ds(1, 8), pl.ds(8, 8), :], lsem.at[0])]
    loads += [pltpu.make_async_copy(saved.at[t], pops.at[t], lsem.at[1 + t]) for t in range(STEPS)]
    loads += [pltpu.make_async_copy(poro, por, lsem.at[4]), pltpu.make_async_copy(fluid, flu, lsem.at[5])]

    barrier = pltpu.get_barrier_semaphore()
    count = jnp.int32(0)
    for off in OFFSETS:
        there = exists(off)

        @pl.when(there)
        def _():
            pl.semaphore_signal(barrier, inc=1, device_id=device(off), device_id_type=pl.DeviceIdType.MESH)

        count = count + there.astype(jnp.int32)

    for i in (0, 3, 2, 1, 4, 5):
        loads[i].start()

    zero = jnp.zeros((8, 128), jnp.float32)
    for off in ((-1, 0, 0), (1, 0, 0)):

        @pl.when(jnp.logical_not(exists(off)))
        def _():
            part = 0 if off[0] < 0 else 9

            def clear(r, _):
                for b, c in PAIRS:
                    for tile in range(3):
                        adj[r, 1 + off[0], b, c, part, pl.ds(8 * tile, 8), :] = zero
                return 0

            lax.fori_loop(0, STEPS, clear, 0)

    for off in ((0, -1, 0), (0, 1, 0)):

        @pl.when(jnp.logical_not(exists(off)))
        def _():
            def clear(n, _):
                r, x = n // 10, n % 10
                for a, c in PAIRS:
                    row = 0 if off[1] < 0 else 16
                    adj[r, a, 1 + off[1], c, x, pl.ds(row, 8), :] = zero
                return 0

            lax.fori_loop(0, STEPS * 10, clear, 0)

    for k, off in enumerate(OFFSETS):
        if off[2]:

            @pl.when(jnp.logical_not(exists(back(off))))
            def _():
                for r in range(STEPS):
                    zrecv[r, k] = zero

    lane = lax.broadcasted_iota(jnp.int32, (8, 128), 1)
    row = lax.broadcasted_iota(jnp.int32, (8, 128), 0)
    group = lane >> 3
    inner = lane & 7
    ymod = jnp.where(group < 3, group, jnp.where(group < 6, group - 3, group - 6))
    xmask = {1: (group < 3) & (inner == 0), -1: (group >= 6) & (inner == 7)}
    ymask = {1: (ymod == 0) & (row == 0), -1: (ymod == 2) & (row == 7)}

    def copies(r):
        made = {}
        for k, (dx, dy, dz) in enumerate(OFFSETS):
            a, b = 1 - dx, 1 - dy
            xs, xd = (8, 0) if dx > 0 else (1, 9)
            ys, yd = (15, 7) if dy > 0 else (8, 16)
            if dz:
                src, dst = ztile.at[r, (1 - dz) // 2], zrecv.at[r, k]
            elif not dx:
                src = adj.at[r, :, b, :, pl.ds(1, 8), pl.ds(ys, 1), :]
                dst = adj.at[r, :, b, :, pl.ds(1, 8), pl.ds(yd, 1), :]
            elif not dy:
                src = adj.at[r, a, :, :, xs, pl.ds(8, 8), :]
                dst = adj.at[r, a, :, :, xd, pl.ds(8, 8), :]
            else:
                src = adj.at[r, a, b, :, xs, pl.ds(ys, 1), :]
                dst = adj.at[r, a, b, :, xd, pl.ds(yd, 1), :]
            off = (dx, dy, dz)
            made[off] = pltpu.make_async_remote_copy(
                src, dst, ssem.at[r, k], rsem.at[r, k],
                device_id=device(off), device_id_type=pl.DeviceIdType.MESH,
            )
        return made

    def pack(tiles, x, value):
        lower, upper = tiles
        for a, b in PAIRS:
            spot = (3 * a + b) * 8 + ((x + 1 - a) & 7)
            here = lane == spot
            upper = jnp.where(here, pltpu.roll(value(a, b, 0), spot + 1, 1), upper)
            lower = jnp.where(here, pltpu.roll(value(a, b, 2), spot, 1), lower)
        return lower, upper

    def shifted(tile):
        return jnp.where(ymod == 1, tile, jnp.where(ymod == 0, pltpu.roll(tile, 1, 0), pltpu.roll(tile, 7, 0)))

    def start(r, tiles):
        ztile[r, 1] = shifted(tiles[0])
        ztile[r, 0] = shifted(tiles[1])
        made = copies(r)
        for off in OFFSETS:
            pl.when(exists(off))(made[off].start)

    def arrive(r):
        made = copies(r)
        for off in OFFSETS:
            pl.when(exists(back(off)))(made[off].wait_recv)

    def edge(r, dz):
        def at(dx, dy):
            return zrecv[r, OFFSETS.index((dx, dy, dz))]

        def line(dx):
            return jnp.where(ymask[1], at(dx, 1), jnp.where(ymask[-1], at(dx, -1), at(dx, 0)))

        return jnp.where(xmask[1], line(1), jnp.where(xmask[-1], line(-1), line(0)))

    loads[0].wait()
    tiles = lax.fori_loop(
        0, 8, lambda x, t: pack(t, x, lambda a, b, c: adj[0, a, b, c, x + 1, pl.ds(8, 8), :]), (zero, zero)
    )
    for t in (2, 1, 0):
        loads[1 + t].wait()

    def prepare(n, _):
        t, x = n // 8, n % 8
        rho, mx, my, mz = f_moments(lambda a, b, c: pops[t, 9 * a + 3 * b + c, x])
        flow[t, 0, x] = rho
        flow[t, 1, x] = mx / rho
        flow[t, 2, x] = my / rho
        flow[t, 3, x] = mz / rho
        return 0

    lax.fori_loop(0, STEPS * 8, prepare, 0)
    loads[4].wait()
    loads[5].wait()

    pl.semaphore_wait(barrier, count)
    start(0, tiles)

    for r in range(STEPS):
        t = STEPS - 1 - r
        last = r == STEPS - 1
        arrive(r)
        above, below = edge(r, -1), edge(r, 1)

        def step(x, tiles):
            p = [[[None] * 3 for _ in range(3)] for _ in range(3)]
            for a, b in PAIRS:
                spot = (3 * a + b) * 8 + x
                low, mid, high = (adj[r, a, b, c, x + a, pl.ds(7 + b, 8), :] for c in range(3))
                low = jnp.where(lane == 0, pltpu.roll(below, (128 - spot) & 127, 1), pltpu.roll(low, 1, 1))
                high = jnp.where(lane == 127, pltpu.roll(above, 127 - spot, 1), pltpu.roll(high, 127, 1))
                p[a][b] = [low, mid, high]
            p0, (px, py, pz), (pxx, pyy, pzz, pxy, pxz, pyz) = weighted_moments(p)
            rho, ux, uy, uz = (flow[t, k, x] for k in range(4))
            is_fluid = flu[x] == 1
            s = jnp.where(is_fluid, por[x], 1.0)
            usq = 1.5 * (ux * ux + uy * uy + uz * uz)
            qx = pxx * ux + pxy * uy + pxz * uz
            qy = pxy * ux + pyy * uy + pyz * uz
            qz = pxz * ux + pyz * uy + pzz * uz
            uq = 4.5 * (ux * qx + uy * qy + uz * qz)
            factor = (1.0 - s) * (1.6 / 216.0)
            base = factor * (p0 + (usq * p0 - uq))
            three = 3.0 * factor
            bx = three * (px - ux * p0 + 3.0 * qx)
            by = three * (py - uy * p0 + 3.0 * qy)
            bz = three * (pz - uz * p0 + 3.0 * qz)
            keep = -0.6 * (1.0 - s)

            total = None
            for a, b in PAIRS:
                for c in range(3):
                    i = 9 * a + 3 * b + c
                    term = p[a][b][c] * (pops[t, 26 - i, x] + 0.6 * pops[t, i, x])
                    total = term if total is None else total + term
            total = total - (1.6 / 216.0) * rho * (p0 - usq * p0 + 3.0 * (px * ux + py * uy + pz * uz) + uq)
            total = jnp.where(is_fluid, total, 0.0)
            acc[x] = total if r == 0 else acc[x] + total

            new = {}
            for a in range(3):
                ga = (base - bx, base, base + bx)[a]
                for b in range(3):
                    gb = (ga - by, ga, ga + by)[b]
                    for c in range(3):
                        g = (gb - bz, gb, gb + bz)[c]
                        value = keep * p[a][b][c] + (s * p[2 - a][2 - b][2 - c] + g)
                        new[a, b, c] = value
                        if last:
                            res[9 * a + 3 * b + c, x] = value
                        else:
                            adj[r + 1, a, b, c, x + 1, pl.ds(8, 8), :] = value
            if last:
                pltpu.make_async_copy(res.at[:, x], out.at[:, x], osem.at[x]).start()
                return tiles
            return pack(tiles, x, lambda a, b, c: new[a, b, c])

        tiles = lax.fori_loop(0, 8, step, (zero, zero))
        if not last:
            start(r + 1, tiles)

    done = pltpu.make_async_copy(acc, grad, osem.at[8])
    done.start()
    for r in range(STEPS):
        made = copies(r)
        for off in OFFSETS:
            pl.when(exists(off))(made[off].wait_send)
    for x in range(8):
        pltpu.make_async_copy(res.at[:, x], out.at[:, x], osem.at[x]).wait()
    done.wait()


def solution(mesh):
    sizes = tuple(mesh.shape[a] for a in AXES)
    f32 = jnp.float32
    call = pl.pallas_call(
        functools.partial(kernel, sizes),
        out_shape=(
            jax.ShapeDtypeStruct((27, 8, 8, 128), f32),
            jax.ShapeDtypeStruct((8, 8, 128), f32),
        ),
        in_specs=[pl.BlockSpec(memory_space=pl.ANY)] * 4,
        out_specs=[pl.BlockSpec(memory_space=pl.ANY)] * 2,
        scratch_shapes=[
            pltpu.VMEM((STEPS, 3, 3, 3, 10, 24, 128), f32),
            pltpu.VMEM((STEPS, 27, 8, 8, 128), f32),
            pltpu.VMEM((STEPS, 4, 8, 8, 128), f32),
            pltpu.VMEM((8, 8, 128), f32),
            pltpu.VMEM((8, 8, 128), jnp.int32),
            pltpu.VMEM((27, 8, 8, 128), f32),
            pltpu.VMEM((8, 8, 128), f32),
            pltpu.VMEM((STEPS, 2, 8, 128), f32),
            pltpu.VMEM((STEPS, 26, 8, 128), f32),
            pltpu.SemaphoreType.DMA((6,)),
            pltpu.SemaphoreType.DMA((9,)),
            pltpu.SemaphoreType.DMA((STEPS, 26)),
            pltpu.SemaphoreType.DMA((STEPS, 26)),
        ],
        compiler_params=pltpu.CompilerParams(
            collective_id=0, has_side_effects=True, vmem_limit_bytes=40 * 1024 * 1024
        ),
    )

    def local(saved, porosity, fluid, seed_adjoint):
        return call(saved, porosity, fluid, seed_adjoint.reshape(3, 3, 3, 8, 8, 128))

    return jax.shard_map(
        local,
        mesh=mesh,
        in_specs=(
            P(None, None, "gx", "gy", "gz"),
            P("gx", "gy", "gz"),
            P("gx", "gy", "gz"),
            P(None, "gx", "gy", "gz"),
        ),
        out_specs=(P(None, "gx", "gy", "gz"), P("gx", "gy", "gz")),
        check_vma=False,
    )
```

profile of v0, /device:TPU:1, one launch (start us, length us, event | category | flops | bytes accessed | tf_op | source)
XLA Modules:
  0.0 33.9 jit_solution(5036134672824220528)
XLA Ops:
  0.6 0.0 copy-start
  0.6 1.7 %copy-done = f32[3,27,8,8,128]{4,3,2,1,0:T(8,128)S(1)} copy-done((f32[3,27,8,8,128]{4,3,2,1,0:T(8,128)S(1)}, f32[3,27,8,8,128]{4,3,2,1,0:T(8,128)}, u32[]{:S(2)}) %copy-start) | copy-done | bytes 2654232
  2.4 0.0 copy-start.1
  2.4 1.2 %copy-done.1 = f32[27,8,8,128]{3,2,1,0:T(8,128)S(1)} copy-done((f32[27,8,8,128]{3,2,1,0:T(8,128)S(1)}, f32[27,8,8,128]{3,2,1,0:T(8,128)}, u32[]{:S(2)}) %copy-start.1) | copy-done | bytes 884760
  3.5 0.0 copy-start.2
  3.6 0.8 %copy-done.2 = f32[8,8,128]{2,1,0:T(8,128)S(1)} copy-done((f32[8,8,128]{2,1,0:T(8,128)S(1)}, f32[8,8,128]{2,1,0:T(8,128)}, u32[]{:S(2)}) %copy-start.2) | copy-done | bytes 32792
  4.3 0.0 copy-start.3
  4.3 0.8 %copy-done.3 = s32[8,8,128]{2,1,0:T(8,128)S(1)} copy-done((s32[8,8,128]{2,1,0:T(8,128)S(1)}, s32[8,8,128]{2,1,0:T(8,128)}, u32[]{:S(2)}) %copy-start.3) | copy-done | bytes 32792
  5.1 27.3 %shard_map.59 = (f32[27,8,8,128]{3,2,1,0:T(8,128)S(1)}, f32[8,8,128]{2,1,0:T(8,128)S(1)}) custom-call(f32[3,27,8,8,128]{4,3,2,1,0:T(8,128)S(1)} %copy-done, f32[8,8,128]{2,1,0:T(8,128)S(1)} %copy-done.2, s32[8,8,128]{2,1,0:T(8,128)S(1)} %copy-done.3, f32[3,3,3,8,8,128]{5,4,3,2,1,0:T(8,128)S(1)} %bitcast.1), custom_call_target="tpu_custom_call" | custom-call | tf_op jit(solution)/shard_map/pallas_call | solution.py:325
  32.4 0.9 %copy.8 = f32[27,8,8,128]{3,2,1,0:T(8,128)} copy(f32[27,8,8,128]{3,2,1,0:T(8,128)S(1)} %get-tuple-element.4) | data formatting | bytes 1769472
  33.3 0.6 %copy.9 = f32[8,8,128]{2,1,0:T(8,128)} copy(f32[8,8,128]{2,1,0:T(8,128)S(1)} %get-tuple-element.5) | data formatting | bytes 65536
Async XLA Ops:
  0.6 1.8 %copy-start = (f32[3,27,8,8,128]{4,3,2,1,0:T(8,128)S(1)}, f32[3,27,8,8,128]{4,3,2,1,0:T(8,128)}, u32[]{:S(2)}) copy-start(f32[3,27,8,8,128]{4,3,2,1,0:T(8,128)} %saved.1) | copy-start | bytes 7962628
  2.4 1.2 %copy-start.1 = (f32[27,8,8,128]{3,2,1,0:T(8,128)S(1)}, f32[27,8,8,128]{3,2,1,0:T(8,128)}, u32[]{:S(2)}) copy-start(f32[27,8,8,128]{3,2,1,0:T(8,128)} %param.7) | copy-start | bytes 2654212
  3.5 0.8 %copy-start.2 = (f32[8,8,128]{2,1,0:T(8,128)S(1)}, f32[8,8,128]{2,1,0:T(8,128)}, u32[]{:S(2)}) copy-start(f32[8,8,128]{2,1,0:T(8,128)} %poro.1) | copy-start | bytes 98308
  4.3 0.8 %copy-start.3 = (s32[8,8,128]{2,1,0:T(8,128)S(1)}, s32[8,8,128]{2,1,0:T(8,128)}, u32[]{:S(2)}) copy-start(s32[8,8,128]{2,1,0:T(8,128)} %fluid.1) | copy-start | bytes 98308
where the time goes:
time: 34.3 us; the launch traced here: 33.9 us
  Pallas kernels  27.3 us (80%)
  local copies, waits for them, and re-layouts  5.95 us (17%)
  between operations  0.65 us (2%)
    pallas_call x1, Pallas kernels, local(): call(saved, porosity, fluid, seed_adjoint.reshape(3, 3, 3, 8, 8, 128))  27.3 us
    unnamed x10, local copies, waits for them, and re-layouts  5.95 us

commit v1 on v0

--- a/solution.py
+++ b/solution.py
@@ -55,8 +55,8 @@
 
 def kernel(
     sizes, saved, poro, fluid, seed, out, grad,
-    adj, pops, flow, por, flu, res, acc, ztile, zrecv,
-    lsem, osem, ssem, rsem,
+    adj, pops, flow, por, flu, ztile, zrecv,
+    lsem, ssem, rsem,
 ):
     me = [lax.axis_index(a) for a in AXES]
 
@@ -255,7 +255,7 @@
                     total = term if total is None else total + term
             total = total - (1.6 / 216.0) * rho * (p0 - usq * p0 + 3.0 * (px * ux + py * uy + pz * uz) + uq)
             total = jnp.where(is_fluid, total, 0.0)
-            acc[x] = total if r == 0 else acc[x] + total
+            grad[x] = total if r == 0 else grad[x] + total
 
             new = {}
             for a in range(3):
@@ -267,27 +267,21 @@
                         value = keep * p[a][b][c] + (s * p[2 - a][2 - b][2 - c] + g)
                         new[a, b, c] = value
                         if last:
-                            res[9 * a + 3 * b + c, x] = value
+                            out[9 * a + 3 * b + c, x] = value
                         else:
                             adj[r + 1, a, b, c, x + 1, pl.ds(8, 8), :] = value
             if last:
-                pltpu.make_async_copy(res.at[:, x], out.at[:, x], osem.at[x]).start()
                 return tiles
             return pack(tiles, x, lambda a, b, c: new[a, b, c])
 
-        tiles = lax.fori_loop(0, 8, step, (zero, zero))
+        tiles = lax.fori_loop(0, 8, step, (zero, zero), unroll=8)
         if not last:
             start(r + 1, tiles)
 
-    done = pltpu.make_async_copy(acc, grad, osem.at[8])
-    done.start()
     for r in range(STEPS):
         made = copies(r)
         for off in OFFSETS:
             pl.when(exists(off))(made[off].wait_send)
-    for x in range(8):
-        pltpu.make_async_copy(res.at[:, x], out.at[:, x], osem.at[x]).wait()
-    done.wait()
 
 
 def solution(mesh):
@@ -296,28 +290,25 @@
     call = pl.pallas_call(
         functools.partial(kernel, sizes),
         out_shape=(
-            jax.ShapeDtypeStruct((27, 8, 8, 128), f32),
-            jax.ShapeDtypeStruct((8, 8, 128), f32),
+            pltpu.VMEM((27, 8, 8, 128), f32),
+            pltpu.VMEM((8, 8, 128), f32),
         ),
-        in_specs=[pl.BlockSpec(memory_space=pl.ANY)] * 4,
-        out_specs=[pl.BlockSpec(memory_space=pl.ANY)] * 2,
+        in_specs=[pl.BlockSpec(memory_space=pltpu.HBM)] * 4,
+        out_specs=[pl.BlockSpec(memory_space=pltpu.VMEM)] * 2,
         scratch_shapes=[
             pltpu.VMEM((STEPS, 3, 3, 3, 10, 24, 128), f32),
             pltpu.VMEM((STEPS, 27, 8, 8, 128), f32),
             pltpu.VMEM((STEPS, 4, 8, 8, 128), f32),
             pltpu.VMEM((8, 8, 128), f32),
             pltpu.VMEM((8, 8, 128), jnp.int32),
-            pltpu.VMEM((27, 8, 8, 128), f32),
-            pltpu.VMEM((8, 8, 128), f32),
             pltpu.VMEM((STEPS, 2, 8, 128), f32),
             pltpu.VMEM((STEPS, 26, 8, 128), f32),
             pltpu.SemaphoreType.DMA((6,)),
-            pltpu.SemaphoreType.DMA((9,)),
             pltpu.SemaphoreType.DMA((STEPS, 26)),
             pltpu.SemaphoreType.DMA((STEPS, 26)),
         ],
         compiler_params=pltpu.CompilerParams(
-            collective_id=0, has_side_effects=True, vmem_limit_bytes=40 * 1024 * 1024
+            collective_id=0, has_side_effects=True, vmem_limit_bytes=60 * 1024 * 1024
         ),
     )
 

time: 34.3 us -> 27.9 us (0.81)
  local copies, waits for them, and re-layouts: 5.95 us -> 1.53 us
  Pallas kernels: 27.3 us -> 25.6 us
    unnamed x10 -> x2, local copies, waits for them, and re-layouts: 5.95 us -> 1.53 us
    pallas_call x1, Pallas kernels: 27.3 us -> 25.6 us  [local(): call(saved, porosity, fluid, seed_adjoint.reshape(3, 3, 3, 8, 8, 128))]
where the time goes in v1:
time: 27.9 us; the launch traced here: 27.8 us
  Pallas kernels  25.6 us (92%)
  local copies, waits for them, and re-layouts  1.53 us (5%)
  between operations  0.64 us (2%)
    pallas_call x1, Pallas kernels, local(): call(saved, porosity, fluid, seed_adjoint.reshape(3, 3, 3, 8, 8, 128))  25.6 us
    unnamed x2, local copies, waits for them, and re-layouts  1.53 us

profile of v1, /device:TPU:1, one launch (start us, length us, event | category | flops | bytes accessed | tf_op | source)
XLA Modules:
  0.0 27.8 jit_solution(562683014640047671)
XLA Ops:
  0.6 25.6 %shard_map.59 = (f32[27,8,8,128]{3,2,1,0:T(8,128)S(1)}, f32[8,8,128]{2,1,0:T(8,128)S(1)}) custom-call(f32[3,27,8,8,128]{4,3,2,1,0:T(8,128)} %saved.1, f32[8,8,128]{2,1,0:T(8,128)} %poro.1, s32[8,8,128]{2,1,0:T(8,128)} %fluid.1, f32[3,3,3,8,8,128]{5,4,3,2,1,0:T(8,128)} %bitcast.1), custom_call_target="tpu_custom_call" | custom-call | tf_op jit(solution)/shard_map/pallas_call | solution.py:316
  26.3 0.9 %copy.8 = f32[27,8,8,128]{3,2,1,0:T(8,128)} copy(f32[27,8,8,128]{3,2,1,0:T(8,128)S(1)} %get-tuple-element.2) | data formatting | bytes 1769472
  27.2 0.6 %copy.9 = f32[8,8,128]{2,1,0:T(8,128)} copy(f32[8,8,128]{2,1,0:T(8,128)S(1)} %get-tuple-element.3) | data formatting | bytes 65536

commit v2 on v1

v2 whole, which is shorter than its diff:
```python
import functools
import itertools

import jax
import jax.numpy as jnp
from jax import lax
from jax.experimental import pallas as pl
from jax.experimental.pallas import tpu as pltpu
from jax.sharding import PartitionSpec as P

STEPS = 3
AXES = ("gx", "gy", "gz")
OFFSETS = sorted(
    (o for o in itertools.product((-1, 0, 1), repeat=3) if any(o)),
    key=lambda o: (not o[1], -sum(map(abs, o))),
)
PAIRS = tuple(itertools.product(range(3), range(3)))


def f_moments(pops):
    s = [[pops(a, b, 0) + pops(a, b, 1) + pops(a, b, 2) for b in range(3)] for a in range(3)]
    dz = [sum(pops(a, b, 2) - pops(a, b, 0) for b in range(3)) for a in range(3)]
    sy = [s[a][0] + s[a][1] + s[a][2] for a in range(3)]
    dy = [s[a][2] - s[a][0] for a in range(3)]
    return (
        sy[0] + sy[1] + sy[2],
        sy[2] - sy[0],
        dy[0] + dy[1] + dy[2],
        dz[0] + dz[1] + dz[2],
    )


def even(v):
    side = v[0] + v[2]
    return 4.0 * v[1] + side, v[2] - v[0], side


def weighted_moments(p):
    z = [[even([p[a][b][c] for c in range(3)]) for b in range(3)] for a in range(3)]
    y = []
    for a in range(3):
        z0, z1, z2 = ([z[a][b][k] for b in range(3)] for k in range(3))
        y00, y10, y20 = even(z0)
        y01, y11, _ = even(z1)
        y02, _, _ = even(z2)
        y.append((y00, y10, y20, y01, y11, y02))
    p0, px, pxx = even([y[a][0] for a in range(3)])
    py, pxy, _ = even([y[a][1] for a in range(3)])
    pyy, _, _ = even([y[a][2] for a in range(3)])
    pz, pxz, _ = even([y[a][3] for a in range(3)])
    pyz, _, _ = even([y[a][4] for a in range(3)])
    pzz, _, _ = even([y[a][5] for a in range(3)])
    return p0, (px, py, pz), (pxx, pyy, pzz, pxy, pxz, pyz)


def positions():
    lane = lax.broadcasted_iota(jnp.int32, (8, 128), 1)
    row = lax.broadcasted_iota(jnp.int32, (8, 128), 0)
    group = lane >> 3
    ymod = jnp.where(group < 3, group, jnp.where(group < 6, group - 3, group - 6))
    return lane, row, group, ymod


def pull(adj, x, edges, lane):
    above, below = edges
    p = [[None] * 3 for _ in range(3)]
    for a, b in PAIRS:
        spot = (3 * a + b) * 8 + x
        low, mid, high = (adj[a, b, c, x + a, pl.ds(7 + b, 8), :] for c in range(3))
        low = jnp.where(lane == 0, pltpu.roll(below, (128 - spot) & 127, 1), pltpu.roll(low, 1, 1))
        high = jnp.where(lane == 127, pltpu.roll(above, 127 - spot, 1), pltpu.roll(high, 127, 1))
        p[a][b] = [low, mid, high]
    return p


def terms(p, flow, x):
    p0, first, (pxx, pyy, pzz, pxy, pxz, pyz) = weighted_moments(p)
    ux, uy, uz = (flow[k, x] for k in (1, 2, 3))
    usq = 1.5 * (ux * ux + uy * uy + uz * uz)
    qx = pxx * ux + pxy * uy + pxz * uz
    qy = pxy * ux + pyy * uy + pyz * uz
    qz = pxz * ux + pyz * uy + pzz * uz
    uq = 4.5 * (ux * qx + uy * qy + uz * qz)
    return p0, first, (ux, uy, uz), usq, (qx, qy, qz), uq


def new_adjoint(p, moments, s, store):
    p0, (px, py, pz), (ux, uy, uz), usq, (qx, qy, qz), uq = moments
    factor = (1.0 - s) * (1.6 / 216.0)
    base = factor * (p0 + (usq * p0 - uq))
    three = 3.0 * factor
    bx = three * (px - ux * p0 + 3.0 * qx)
    by = three * (py - uy * p0 + 3.0 * qy)
    bz = three * (pz - uz * p0 + 3.0 * qz)
    keep = -0.6 * (1.0 - s)
    for a in range(3):
        ga = (base - bx, base, base + bx)[a]
        for b in range(3):
            gb = (ga - by, ga, ga + by)[b]
            for c in range(3):
                g = (gb - bz, gb, gb + bz)[c]
                store(a, b, c, keep * p[a][b][c] + (s * p[2 - a][2 - b][2 - c] + g))


def porosity_term(p, moments, rho, pops, x):
    p0, (px, py, pz), (ux, uy, uz), usq, _, uq = moments
    total = None
    for a, b in PAIRS:
        for c in range(3):
            i = 9 * a + 3 * b + c
            term = p[a][b][c] * (pops[26 - i, x] + 0.6 * pops[i, x])
            total = term if total is None else total + term
    return total - (1.6 / 216.0) * rho * (p0 - usq * p0 + 3.0 * (px * ux + py * uy + pz * uz) + uq)


def last_kernel(adj, edges, pops, flow, por, flu, acc, out, grad, res, total, sem):
    lane = positions()[0]
    sides = edges[0], edges[1]
    for x in range(8):
        p = pull(adj, x, sides, lane)
        moments = terms(p, flow, x)
        is_fluid = flu[x] == 1

        def store(a, b, c, value):
            res[9 * a + 3 * b + c, x] = value

        new_adjoint(p, moments, jnp.where(is_fluid, por[x], 1.0), store)
        pltpu.make_async_copy(res.at[:, x], out.at[:, x], sem.at[x]).start()
        total[x] = acc[x] + jnp.where(is_fluid, porosity_term(p, moments, flow[0, x], pops, x), 0.0)
    done = pltpu.make_async_copy(total, grad, sem.at[8])
    done.start()
    for x in range(8):
        pltpu.make_async_copy(res.at[:, x], out.at[:, x], sem.at[x]).wait()
    done.wait()


def kernel(
    sizes, saved, poro, fluid, seed,
    adj2, edges, pops0, flow0, por, flu, acc,
    adj01, pops12, flow12, ztile, zrecv,
    lsem, ssem, rsem,
):
    adjs = (adj01.at[0], adj01.at[1], adj2)
    pops = (pops0, pops12.at[0], pops12.at[1])
    flow = (flow0, flow12.at[0], flow12.at[1])
    me = [lax.axis_index(a) for a in AXES]

    def exists(off):
        found = None
        for i, o in enumerate(off):
            if o:
                here = me[i] < sizes[i] - 1 if o > 0 else me[i] > 0
                found = here if found is None else jnp.logical_and(found, here)
        return found

    def device(off):
        return tuple(m + o for m, o in zip(me, off))

    def back(off):
        return tuple(-o for o in off)

    loads = [pltpu.make_async_copy(seed, adjs[0].at[:, :, :, pl.ds(1, 8), pl.ds(8, 8), :], lsem.at[0])]
    loads += [pltpu.make_async_copy(saved.at[t], pops[t], lsem.at[1 + t]) for t in range(STEPS)]
    loads += [pltpu.make_async_copy(poro, por, lsem.at[4]), pltpu.make_async_copy(fluid, flu, lsem.at[5])]

    barrier = pltpu.get_barrier_semaphore()
    count = jnp.int32(0)
    for off in OFFSETS:
        there = exists(off)

        @pl.when(there)
        def _():
            pl.semaphore_signal(barrier, inc=1, device_id=device(off), device_id_type=pl.DeviceIdType.MESH)

        count = count + there.astype(jnp.int32)

    for i in (0, 3, 2, 1, 4, 5):
        loads[i].start()

    zero = jnp.zeros((8, 128), jnp.float32)
    for off in ((-1, 0, 0), (1, 0, 0)):

        @pl.when(jnp.logical_not(exists(off)))
        def _():
            part = 0 if off[0] < 0 else 9

            for adj in adjs:
                for b, c in PAIRS:
                    for tile in range(3):
                        adj[1 + off[0], b, c, part, pl.ds(8 * tile, 8), :] = zero

    for off in ((0, -1, 0), (0, 1, 0)):

        @pl.when(jnp.logical_not(exists(off)))
        def _():
            def clear(x, _):
                for adj in adjs:
                    for a, c in PAIRS:
                        adj[a, 1 + off[1], c, x, pl.ds(0 if off[1] < 0 else 16, 8), :] = zero
                return 0

            lax.fori_loop(0, 10, clear, 0)

    for k, off in enumerate(OFFSETS):
        if off[2]:

            @pl.when(jnp.logical_not(exists(back(off))))
            def _():
                for r in range(STEPS):
                    zrecv[r, k] = zero

    lane, row, group, ymod = positions()
    inner = lane & 7
    xmask = {1: (group < 3) & (inner == 0), -1: (group >= 6) & (inner == 7)}
    ymask = {1: (ymod == 0) & (row == 0), -1: (ymod == 2) & (row == 7)}

    def copies(r):
        made = {}
        for k, (dx, dy, dz) in enumerate(OFFSETS):
            a, b = 1 - dx, 1 - dy
            xs, xd = (8, 0) if dx > 0 else (1, 9)
            ys, yd = (15, 7) if dy > 0 else (8, 16)
            if dz:
                rows = pl.ds(7 * b // 2, 1) if dy else pl.ds(0, 8)
                src, dst = ztile.at[r, (1 - dz) // 2, rows], zrecv.at[r, k, rows]
            elif not dx:
                src = adjs[r].at[:, b, :, pl.ds(1, 8), pl.ds(ys, 1), :]
                dst = adjs[r].at[:, b, :, pl.ds(1, 8), pl.ds(yd, 1), :]
            elif not dy:
                src = adjs[r].at[a, :, :, xs, pl.ds(8, 8), :]
                dst = adjs[r].at[a, :, :, xd, pl.ds(8, 8), :]
            else:
                src = adjs[r].at[a, b, :, xs, pl.ds(ys, 1), :]
                dst = adjs[r].at[a, b, :, xd, pl.ds(yd, 1), :]
            off = (dx, dy, dz)
            made[off] = pltpu.make_async_remote_copy(
                src, dst, ssem.at[r, k], rsem.at[r, k],
                device_id=device(off), device_id_type=pl.DeviceIdType.MESH,
            )
        return made

    def pack(tiles, x, value):
        lower, upper = tiles
        for a, b in PAIRS:
            spot = (3 * a + b) * 8 + ((x + 1 - a) & 7)
            here = lane == spot
            upper = jnp.where(here, pltpu.roll(value(a, b, 0), spot + 1, 1), upper)
            lower = jnp.where(here, pltpu.roll(value(a, b, 2), spot, 1), lower)
        return lower, upper

    def shifted(tile):
        return jnp.where(ymod == 1, tile, jnp.where(ymod == 0, pltpu.roll(tile, 1, 0), pltpu.roll(tile, 7, 0)))

    def start(r, tiles):
        ztile[r, 1] = shifted(tiles[0])
        ztile[r, 0] = shifted(tiles[1])
        made = copies(r)
        for off in OFFSETS:
            pl.when(exists(off))(made[off].start)

    def arrive(r):
        made = copies(r)
        for off in reversed(OFFSETS):
            pl.when(exists(back(off)))(made[off].wait_recv)

    def edge(r, dz):
        def at(dx, dy):
            return zrecv[r, OFFSETS.index((dx, dy, dz))]

        def line(dx):
            return jnp.where(ymask[1], at(dx, 1), jnp.where(ymask[-1], at(dx, -1), at(dx, 0)))

        return jnp.where(xmask[1], line(1), jnp.where(xmask[-1], line(-1), line(0)))

    loads[0].wait()
    tiles = lax.fori_loop(
        0, 8, lambda x, t: pack(t, x, lambda a, b, c: adjs[0][a, b, c, x + 1, pl.ds(8, 8), :]), (zero, zero)
    )
    for t in (2, 1, 0):
        loads[1 + t].wait()

    def prepare(x, _):
        for t in range(STEPS):
            rho, mx, my, mz = f_moments(lambda a, b, c: pops[t][9 * a + 3 * b + c, x])
            flow[t][0, x] = rho
            flow[t][1, x] = mx / rho
            flow[t][2, x] = my / rho
            flow[t][3, x] = mz / rho
        return 0

    lax.fori_loop(0, 8, prepare, 0)
    loads[4].wait()
    loads[5].wait()

    pl.semaphore_wait(barrier, count)
    start(0, tiles)

    for r in range(STEPS - 1):
        t = STEPS - 1 - r
        arrive(r)
        sides = edge(r, -1), edge(r, 1)

        def step(x, tiles):
            p = pull(adjs[r], x, sides, lane)
            new = {}

            def store(a, b, c, value):
                new[a, b, c] = value
                adjs[r + 1][a, b, c, x + 1, pl.ds(8, 8), :] = value

            new_adjoint(p, terms(p, flow[t], x), jnp.where(flu[x] == 1, por[x], 1.0), store)
            return pack(tiles, x, lambda a, b, c: new[a, b, c])

        start(r + 1, lax.fori_loop(0, 8, step, (zero, zero), unroll=8))

        def gradient(x, _):
            p = pull(adjs[r], x, sides, lane)
            term = porosity_term(p, terms(p, flow[t], x), flow[t][0, x], pops[t], x)
            term = jnp.where(flu[x] == 1, term, 0.0)
            acc[x] = term if r == 0 else acc[x] + term
            return 0

        lax.fori_loop(0, 8, gradient, 0)

    arrive(STEPS - 1)
    edges[0] = edge(STEPS - 1, -1)
    edges[1] = edge(STEPS - 1, 1)
    for r in range(STEPS):
        made = copies(r)
        for off in OFFSETS:
            pl.when(exists(off))(made[off].wait_send)


def solution(mesh):
    sizes = tuple(mesh.shape[a] for a in AXES)
    f32 = jnp.float32
    vmem, tiles = pl.BlockSpec(memory_space=pltpu.VMEM), (8, 8, 128)
    between = (
        pltpu.VMEM((3, 3, 3, 10, 24, 128), f32),
        pltpu.VMEM((2, 8, 128), f32),
        pltpu.VMEM((27, *tiles), f32),
        pltpu.VMEM((4, *tiles), f32),
        pltpu.VMEM(tiles, f32),
        pltpu.VMEM(tiles, jnp.int32),
        pltpu.VMEM(tiles, f32),
    )
    exchange = pl.pallas_call(
        functools.partial(kernel, sizes),
        out_shape=between,
        in_specs=[pl.BlockSpec(memory_space=pltpu.HBM)] * 4,
        out_specs=[vmem] * len(between),
        scratch_shapes=[
            pltpu.VMEM((2, 3, 3, 3, 10, 24, 128), f32),
            pltpu.VMEM((2, 27, *tiles), f32),
            pltpu.VMEM((2, 4, *tiles), f32),
            pltpu.VMEM((STEPS, 2, 8, 128), f32),
            pltpu.VMEM((STEPS, 26, 8, 128), f32),
            pltpu.SemaphoreType.DMA((6,)),
            pltpu.SemaphoreType.DMA((STEPS, 26)),
            pltpu.SemaphoreType.DMA((STEPS, 26)),
        ],
        compiler_params=pltpu.CompilerParams(
            collective_id=0, has_side_effects=True, vmem_limit_bytes=56 * 1024 * 1024
        ),
    )
    last = pl.pallas_call(
        last_kernel,
        out_shape=(jax.ShapeDtypeStruct((27, *tiles), f32), jax.ShapeDtypeStruct(tiles, f32)),
        in_specs=[vmem] * len(between),
        out_specs=[pl.BlockSpec(memory_space=pltpu.HBM)] * 2,
        scratch_shapes=[
            pltpu.VMEM((27, *tiles), f32),
            pltpu.VMEM(tiles, f32),
            pltpu.SemaphoreType.DMA((9,)),
        ],
        compiler_params=pltpu.CompilerParams(vmem_limit_bytes=48 * 1024 * 1024),
    )

    def local(saved, porosity, fluid, seed_adjoint):
        return last(*exchange(saved, porosity, fluid, seed_adjoint.reshape(3, 3, 3, 8, 8, 128)))

    return jax.shard_map(
        local,
        mesh=mesh,
        in_specs=(
            P(None, None, "gx", "gy", "gz"),
            P("gx", "gy", "gz"),
            P("gx", "gy", "gz"),
            P(None, "gx", "gy", "gz"),
        ),
        out_specs=(P(None, "gx", "gy", "gz"), P("gx", "gy", "gz")),
        check_vma=False,
    )
```

time: 27.9 us -> 25.3 us (0.907)
  local copies, waits for them, and re-layouts: 1.53 us -> 0 us
  Pallas kernels: 25.6 us -> 24.6 us
    unnamed x2 -> x0, local copies, waits for them, and re-layouts: 1.53 us -> none
    pallas_call x1 -> x2, Pallas kernels: 25.6 us -> 24.6 us  [the longest x1 23.3 us: local(): exchange(saved, porosity, fluid, seed_adjoint.reshape(3, 3, 3, 8, 8, 128))]
where the time goes in v2:
time: 25.3 us; the launch traced here: 25.2 us
  Pallas kernels  24.6 us (97%)
  between operations  0.64 us (3%)
    pallas_call x1, Pallas kernels, local(): exchange(saved, porosity, fluid, seed_adjoint.reshape(3, 3, 3, 8, 8, 128))  23.3 us
    pallas_call x1, Pallas kernels, local(): last(*exchange(saved, porosity, fluid, seed_adjoint.reshape(3, 3, 3, 8, 8...  1.31 us

profile of v2, /device:TPU:1, one launch (start us, length us, event | category | flops | bytes accessed | tf_op | source)
XLA Modules:
  0.0 25.2 jit_solution(6710317971497072932)
XLA Ops:
  0.6 23.3 %shard_map.59 = (f32[3,3,3,10,24,128]{5,4,3,2,1,0:T(8,128)S(1)}, f32[2,8,128]{2,1,0:T(8,128)S(1)}, f32[27,8,8,128]{3,2,1,0:T(8,128)S(1)}, f32[4,8,8,128]{3,2,1,0...) custom-call(f32[3,27,8,8,128]{4,3,2,1,0:T(8,128)} %saved.1, ...), custom_call_target="tpu_custom_call" | custom-call | tf_op jit(solution)/shard_map/pallas_call | solution.py:380
  23.9 1.3 %shard_map.60 = (f32[27,8,8,128]{3,2,1,0:T(8,128)}, f32[8,8,128]{2,1,0:T(8,128)}) custom-call(f32[3,3,3,10,24,128]{5,4,3,2,1,0:T(8,128)S(1)} %get-tuple-element.9.adj, f32[2,8,128]{2,1,0:T(8,128)S(1)} %get-tuple-element.10.edges, f32[27,8,8,128]{3,2,1,0:T(8,128)S(1)} %get-tuple-element.11.pops, f32[4,8,8,128]{3,2,1,0:T(8,128)S(1)} %get-tuple-element.12.flow, ...), custom_call_target="tpu_custom_call" | custom-call | tf_op jit(solution)/shard_map/pallas_call | solution.py:380

commit v3 on v2

--- a/solution.py
+++ b/solution.py
@@ -61,21 +61,25 @@
     return lane, row, group, ymod
 
 
-def pull(adj, x, edges, lane):
+def pull(read, shift, edges, lane):
     above, below = edges
     p = [[None] * 3 for _ in range(3)]
     for a, b in PAIRS:
-        spot = (3 * a + b) * 8 + x
-        low, mid, high = (adj[a, b, c, x + a, pl.ds(7 + b, 8), :] for c in range(3))
+        spot = (3 * a + b) * 8 + shift
+        low, mid, high = (read(a, b, c) for c in range(3))
         low = jnp.where(lane == 0, pltpu.roll(below, (128 - spot) & 127, 1), pltpu.roll(low, 1, 1))
         high = jnp.where(lane == 127, pltpu.roll(above, 127 - spot, 1), pltpu.roll(high, 127, 1))
         p[a][b] = [low, mid, high]
     return p
 
 
-def terms(p, flow, x):
+def slice_of(adj, x):
+    return lambda a, b, c: adj[a, b, c, x + a, pl.ds(7 + b, 8), :]
+
+
+def terms(p, velocity):
     p0, first, (pxx, pyy, pzz, pxy, pxz, pyz) = weighted_moments(p)
-    ux, uy, uz = (flow[k, x] for k in (1, 2, 3))
+    ux, uy, uz = velocity
     usq = 1.5 * (ux * ux + uy * uy + uz * uz)
     qx = pxx * ux + pxy * uy + pxz * uz
     qy = pxy * ux + pyy * uy + pyz * uz
@@ -84,7 +88,7 @@
     return p0, first, (ux, uy, uz), usq, (qx, qy, qz), uq
 
 
-def new_adjoint(p, moments, s, store):
+def new_adjoint(p, moments, s, store, only=(0, 1, 2)):
     p0, (px, py, pz), (ux, uy, uz), usq, (qx, qy, qz), uq = moments
     factor = (1.0 - s) * (1.6 / 216.0)
     base = factor * (p0 + (usq * p0 - uq))
@@ -95,7 +99,7 @@
     keep = -0.6 * (1.0 - s)
     for a in range(3):
         ga = (base - bx, base, base + bx)[a]
-        for b in range(3):
+        for b in only:
             gb = (ga - by, ga, ga + by)[b]
             for c in range(3):
                 g = (gb - bz, gb, gb + bz)[c]
@@ -117,8 +121,8 @@
     lane = positions()[0]
     sides = edges[0], edges[1]
     for x in range(8):
-        p = pull(adj, x, sides, lane)
-        moments = terms(p, flow, x)
+        p = pull(slice_of(adj, x), x, sides, lane)
+        moments = terms(p, [flow[k, x] for k in (1, 2, 3)])
         is_fluid = flu[x] == 1
 
         def store(a, b, c, value):
@@ -137,7 +141,7 @@
 def kernel(
     sizes, saved, poro, fluid, seed,
     adj2, edges, pops0, flow0, por, flu, acc,
-    adj01, pops12, flow12, ztile, zrecv,
+    adj01, pops12, flow12, ztile, zrecv, plane, zrow,
     lsem, ssem, rsem,
 ):
     adjs = (adj01.at[0], adj01.at[1], adj2)
@@ -223,15 +227,21 @@
             if dz:
                 rows = pl.ds(7 * b // 2, 1) if dy else pl.ds(0, 8)
                 src, dst = ztile.at[r, (1 - dz) // 2, rows], zrecv.at[r, k, rows]
+                if dy and r:
+                    src = zrow.at[r - 1, b // 2, (1 - dz) // 2, rows]
             elif not dx:
-                src = adjs[r].at[:, b, :, pl.ds(1, 8), pl.ds(ys, 1), :]
-                dst = adjs[r].at[:, b, :, pl.ds(1, 8), pl.ds(yd, 1), :]
+                src = adjs[r].at[:, b, :, pl.ds(1, 8), ys, :]
+                dst = adjs[r].at[:, b, :, pl.ds(1, 8), yd, :]
+                if r:
+                    src = plane.at[r - 1, b // 2]
             elif not dy:
                 src = adjs[r].at[a, :, :, xs, pl.ds(8, 8), :]
                 dst = adjs[r].at[a, :, :, xd, pl.ds(8, 8), :]
             else:
                 src = adjs[r].at[a, b, :, xs, pl.ds(ys, 1), :]
                 dst = adjs[r].at[a, b, :, xd, pl.ds(yd, 1), :]
+                if r:
+                    src = plane.at[r - 1, b // 2, a, :, pl.ds(xs - 1, 1), :]
             off = (dx, dy, dz)
             made[off] = pltpu.make_async_remote_copy(
                 src, dst, ssem.at[r, k], rsem.at[r, k],
@@ -251,17 +261,59 @@
     def shifted(tile):
         return jnp.where(ymod == 1, tile, jnp.where(ymod == 0, pltpu.roll(tile, 1, 0), pltpu.roll(tile, 7, 0)))
 
-    def start(r, tiles):
+    def fill(r, tiles):
         ztile[r, 1] = shifted(tiles[0])
         ztile[r, 0] = shifted(tiles[1])
+
+    def start(r, offsets):
         made = copies(r)
-        for off in OFFSETS:
+        for off in offsets:
             pl.when(exists(off))(made[off].start)
+
+    far = [off for off in OFFSETS if off[1]]
+    near = [off for off in OFFSETS if not off[1]]
+
+    def along(tile, y):
+        v = jnp.where(inner == row, jnp.broadcast_to(tile[y : y + 1], (8, 128)), 0.0)
+        for n in (127, 126, 124):
+            v = v + pltpu.roll(v, n, 1)
+        return v
+
+    def outer_plane(r, t, y, sides):
+        flat = adjs[r].reshape(6480, 128)
+        rates = flow[t].reshape(256, 128)
+        there = pl.ds(y, 8, stride=8)
+        p = pull(
+            lambda a, b, c: flat[pl.ds(((9 * a + 3 * b + c) * 10 + a) * 24 + 7 + b + y, 8, stride=24), :],
+            0, [along(side, y) for side in sides], lane,
+        )
+        s = jnp.where(flu.reshape(64, 128)[there, :] == 1, por.reshape(64, 128)[there, :], 1.0)
+        b = 0 if y else 2
+        new = {}
+
+        def store(a, _, c, value):
+            new[a, c] = value
+            plane[r, b // 2, a, c] = value
+
+        new_adjoint(p, terms(p, [rates[pl.ds(64 * k + y, 8, stride=8), :] for k in (1, 2, 3)]), s, store, (b,))
+        for c, edge_lane in ((2, 0), (0, 127)):
+            packed = zero
+            for a in range(3):
+                here = lane == (3 * a + b) * 8 + ((row + 1 - a) & 7)
+                packed = jnp.where(here, jnp.broadcast_to(new[a, c][:, edge_lane : edge_lane + 1], (8, 128)), packed)
+            for n in (4, 2, 1):
+                packed = packed + pltpu.roll(packed, n, 0)
+            zrow[r, b // 2, c // 2] = packed
 
     def arrive(r):
         made = copies(r)
         for off in reversed(OFFSETS):
             pl.when(exists(back(off)))(made[off].wait_recv)
+
+    def leave(r):
+        made = copies(r)
+        for off in OFFSETS:
+            pl.when(exists(off))(made[off].wait_send)
 
     def edge(r, dz):
         def at(dx, dy):
@@ -292,43 +344,47 @@
     loads[4].wait()
     loads[5].wait()
 
+    fill(0, tiles)
     pl.semaphore_wait(barrier, count)
-    start(0, tiles)
+    start(0, OFFSETS)
 
     for r in range(STEPS - 1):
         t = STEPS - 1 - r
         arrive(r)
         sides = edge(r, -1), edge(r, 1)
 
+        outer_plane(r, t, 0, sides)
+        outer_plane(r, t, 7, sides)
+        start(r + 1, far)
+
         def step(x, tiles):
-            p = pull(adjs[r], x, sides, lane)
+            p = pull(slice_of(adjs[r], x), x, sides, lane)
             new = {}
 
             def store(a, b, c, value):
                 new[a, b, c] = value
                 adjs[r + 1][a, b, c, x + 1, pl.ds(8, 8), :] = value
 
-            new_adjoint(p, terms(p, flow[t], x), jnp.where(flu[x] == 1, por[x], 1.0), store)
+            new_adjoint(p, terms(p, [flow[t][k, x] for k in (1, 2, 3)]), jnp.where(flu[x] == 1, por[x], 1.0), store)
             return pack(tiles, x, lambda a, b, c: new[a, b, c])
 
-        start(r + 1, lax.fori_loop(0, 8, step, (zero, zero), unroll=8))
+        fill(r + 1, lax.fori_loop(0, 8, step, (zero, zero), unroll=8))
+        start(r + 1, near)
 
         def gradient(x, _):
-            p = pull(adjs[r], x, sides, lane)
-            term = porosity_term(p, terms(p, flow[t], x), flow[t][0, x], pops[t], x)
+            p = pull(slice_of(adjs[r], x), x, sides, lane)
+            term = porosity_term(p, terms(p, [flow[t][k, x] for k in (1, 2, 3)]), flow[t][0, x], pops[t], x)
             term = jnp.where(flu[x] == 1, term, 0.0)
             acc[x] = term if r == 0 else acc[x] + term
             return 0
 
         lax.fori_loop(0, 8, gradient, 0)
-
+        leave(r)
+
+    leave(STEPS - 1)
     arrive(STEPS - 1)
     edges[0] = edge(STEPS - 1, -1)
     edges[1] = edge(STEPS - 1, 1)
-    for r in range(STEPS):
-        made = copies(r)
-        for off in OFFSETS:
-            pl.when(exists(off))(made[off].wait_send)
 
 
 def solution(mesh):
@@ -355,6 +411,8 @@
             pltpu.VMEM((2, 4, *tiles), f32),
             pltpu.VMEM((STEPS, 2, 8, 128), f32),
             pltpu.VMEM((STEPS, 26, 8, 128), f32),
+            pltpu.VMEM((2, 2, 3, 3, 8, 128), f32),
+            pltpu.VMEM((2, 2, 2, 8, 128), f32),
             pltpu.SemaphoreType.DMA((6,)),
             pltpu.SemaphoreType.DMA((STEPS, 26)),
             pltpu.SemaphoreType.DMA((STEPS, 26)),

time: 25.3 us -> 24.5 us (0.968)
  Pallas kernels: 24.6 us -> 23.7 us
    pallas_call x1, Pallas kernels: 23.3 us -> 22.4 us  [local(): exchange(saved, porosity, fluid, seed_adjoint.reshape(3, 3, 3, 8, 8, 128))]
where the time goes in v3:
time: 24.5 us; the launch traced here: 24.3 us
  Pallas kernels  23.7 us (97%)
  between operations  0.64 us (3%)
    pallas_call x1, Pallas kernels, local(): exchange(saved, porosity, fluid, seed_adjoint.reshape(3, 3, 3, 8, 8, 128))  22.4 us
    pallas_call x1, Pallas kernels, local(): last(*exchange(saved, porosity, fluid, seed_adjoint.reshape(3, 3, 3, 8, 8...  1.31 us

profile of v3, /device:TPU:1, one launch (start us, length us, event | category | flops | bytes accessed | tf_op | source)
XLA Modules:
  0.0 24.3 jit_solution(5827610310954476034)
XLA Ops:
  0.6 22.4 %shard_map.59 = (f32[3,3,3,10,24,128]{5,4,3,2,1,0:T(8,128)S(1)}, f32[2,8,128]{2,1,0:T(8,128)S(1)}, f32[27,8,8,128]{3,2,1,0:T(8,128)S(1)}, f32[4,8,8,128]{3,2,1,0...) custom-call(f32[3,27,8,8,128]{4,3,2,1,0:T(8,128)} %saved.1, ...), custom_call_target="tpu_custom_call" | custom-call | tf_op jit(solution)/shard_map/pallas_call | solution.py:438
  23.0 1.3 %shard_map.60 = (f32[27,8,8,128]{3,2,1,0:T(8,128)}, f32[8,8,128]{2,1,0:T(8,128)}) custom-call(f32[3,3,3,10,24,128]{5,4,3,2,1,0:T(8,128)S(1)} %get-tuple-element.9.adj, f32[2,8,128]{2,1,0:T(8,128)S(1)} %get-tuple-element.10.edges, f32[27,8,8,128]{3,2,1,0:T(8,128)S(1)} %get-tuple-element.11.pops, f32[4,8,8,128]{3,2,1,0:T(8,128)S(1)} %get-tuple-element.12.flow, ...), custom_call_target="tpu_custom_call" | custom-call | tf_op jit(solution)/shard_map/pallas_call | solution.py:438

commit v4 on v3

--- a/solution.py
+++ b/solution.py
@@ -12,7 +12,7 @@
 AXES = ("gx", "gy", "gz")
 OFFSETS = sorted(
     (o for o in itertools.product((-1, 0, 1), repeat=3) if any(o)),
-    key=lambda o: (not o[1], -sum(map(abs, o))),
+    key=lambda o: (not o[1], bool(o[0] or o[2]), not o[2], bool(o[0])),
 )
 PAIRS = tuple(itertools.product(range(3), range(3)))
 
@@ -67,8 +67,12 @@
     for a, b in PAIRS:
         spot = (3 * a + b) * 8 + shift
         low, mid, high = (read(a, b, c) for c in range(3))
-        low = jnp.where(lane == 0, pltpu.roll(below, (128 - spot) & 127, 1), pltpu.roll(low, 1, 1))
-        high = jnp.where(lane == 127, pltpu.roll(above, 127 - spot, 1), pltpu.roll(high, 127, 1))
+        if isinstance(below, list):
+            lowest, highest = below[3 * a + b], above[3 * a + b]
+        else:
+            lowest, highest = pltpu.roll(below, (128 - spot) & 127, 1), pltpu.roll(above, 127 - spot, 1)
+        low = jnp.where(lane == 0, lowest, pltpu.roll(low, 1, 1))
+        high = jnp.where(lane == 127, highest, pltpu.roll(high, 127, 1))
         p[a][b] = [low, mid, high]
     return p
 
@@ -275,9 +279,7 @@
 
     def along(tile, y):
         v = jnp.where(inner == row, jnp.broadcast_to(tile[y : y + 1], (8, 128)), 0.0)
-        for n in (127, 126, 124):
-            v = v + pltpu.roll(v, n, 1)
-        return v
+        return [jnp.sum(jnp.where(group == k, v, 0.0), axis=1, keepdims=True) for k in range(9)]
 
     def outer_plane(r, t, y, sides):
         flat = adjs[r].reshape(6480, 128)

time: 24.5 us -> 23.8 us (0.971)
  Pallas kernels: 23.7 us -> 23.1 us
    pallas_call x1, Pallas kernels: 22.4 us -> 21.8 us  [local(): exchange(saved, porosity, fluid, seed_adjoint.reshape(3, 3, 3, 8, 8, 128))]
where the time goes in v4:
time: 23.8 us; the launch traced here: 23.7 us
  Pallas kernels  23.1 us (97%)
  between operations  0.64 us (3%)
    pallas_call x1, Pallas kernels, local(): exchange(saved, porosity, fluid, seed_adjoint.reshape(3, 3, 3, 8, 8, 128))  21.8 us
    pallas_call x1, Pallas kernels, local(): last(*exchange(saved, porosity, fluid, seed_adjoint.reshape(3, 3, 3, 8, 8...  1.31 us

profile of v4, /device:TPU:1, one launch (start us, length us, event | category | flops | bytes accessed | tf_op | source)
XLA Modules:
  0.0 23.7 jit_solution(6333796241932126293)
XLA Ops:
  0.6 21.8 %shard_map.59 = (f32[3,3,3,10,24,128]{5,4,3,2,1,0:T(8,128)S(1)}, f32[2,8,128]{2,1,0:T(8,128)S(1)}, f32[27,8,8,128]{3,2,1,0:T(8,128)S(1)}, f32[4,8,8,128]{3,2,1,0...) custom-call(f32[3,27,8,8,128]{4,3,2,1,0:T(8,128)} %saved.1, ...), custom_call_target="tpu_custom_call" | custom-call | tf_op jit(solution)/shard_map/pallas_call | solution.py:440
  22.4 1.3 %shard_map.60 = (f32[27,8,8,128]{3,2,1,0:T(8,128)}, f32[8,8,128]{2,1,0:T(8,128)}) custom-call(f32[3,3,3,10,24,128]{5,4,3,2,1,0:T(8,128)S(1)} %get-tuple-element.9.adj, f32[2,8,128]{2,1,0:T(8,128)S(1)} %get-tuple-element.10.edges, f32[27,8,8,128]{3,2,1,0:T(8,128)S(1)} %get-tuple-element.11.pops, f32[4,8,8,128]{3,2,1,0:T(8,128)S(1)} %get-tuple-element.12.flow, ...), custom_call_target="tpu_custom_call" | custom-call | tf_op jit(solution)/shard_map/pallas_call | solution.py:440

commit v5 on v4

--- a/solution.py
+++ b/solution.py
@@ -186,37 +186,6 @@
         loads[i].start()
 
     zero = jnp.zeros((8, 128), jnp.float32)
-    for off in ((-1, 0, 0), (1, 0, 0)):
-
-        @pl.when(jnp.logical_not(exists(off)))
-        def _():
-            part = 0 if off[0] < 0 else 9
-
-            for adj in adjs:
-                for b, c in PAIRS:
-                    for tile in range(3):
-                        adj[1 + off[0], b, c, part, pl.ds(8 * tile, 8), :] = zero
-
-    for off in ((0, -1, 0), (0, 1, 0)):
-
-        @pl.when(jnp.logical_not(exists(off)))
-        def _():
-            def clear(x, _):
-                for adj in adjs:
-                    for a, c in PAIRS:
-                        adj[a, 1 + off[1], c, x, pl.ds(0 if off[1] < 0 else 16, 8), :] = zero
-                return 0
-
-            lax.fori_loop(0, 10, clear, 0)
-
-    for k, off in enumerate(OFFSETS):
-        if off[2]:
-
-            @pl.when(jnp.logical_not(exists(back(off))))
-            def _():
-                for r in range(STEPS):
-                    zrecv[r, k] = zero
-
     lane, row, group, ymod = positions()
     inner = lane & 7
     xmask = {1: (group < 3) & (inner == 0), -1: (group >= 6) & (inner == 7)}
@@ -328,8 +297,44 @@
 
     loads[0].wait()
     tiles = lax.fori_loop(
-        0, 8, lambda x, t: pack(t, x, lambda a, b, c: adjs[0][a, b, c, x + 1, pl.ds(8, 8), :]), (zero, zero)
-    )
+        0, 8, lambda x, t: pack(t, x, lambda a, b, c: adjs[0][a, b, c, x + 1, pl.ds(8, 8), :]), (zero, zero),
+        unroll=8,
+    )
+    fill(0, tiles)
+    pl.semaphore_wait(barrier, count)
+    start(0, OFFSETS)
+
+    for off in ((-1, 0, 0), (1, 0, 0)):
+
+        @pl.when(jnp.logical_not(exists(off)))
+        def _():
+            part = 0 if off[0] < 0 else 9
+
+            for adj in adjs:
+                for b, c in PAIRS:
+                    for tile in range(3):
+                        adj[1 + off[0], b, c, part, pl.ds(8 * tile, 8), :] = zero
+
+    for off in ((0, -1, 0), (0, 1, 0)):
+
+        @pl.when(jnp.logical_not(exists(off)))
+        def _():
+            def clear(x, _):
+                for adj in adjs:
+                    for a, c in PAIRS:
+                        adj[a, 1 + off[1], c, x, pl.ds(0 if off[1] < 0 else 16, 8), :] = zero
+                return 0
+
+            lax.fori_loop(0, 10, clear, 0)
+
+    for k, off in enumerate(OFFSETS):
+        if off[2]:
+
+            @pl.when(jnp.logical_not(exists(back(off))))
+            def _():
+                for r in range(STEPS):
+                    zrecv[r, k] = zero
+
     for t in (2, 1, 0):
         loads[1 + t].wait()
 
@@ -345,10 +350,6 @@
     lax.fori_loop(0, 8, prepare, 0)
     loads[4].wait()
     loads[5].wait()
-
-    fill(0, tiles)
-    pl.semaphore_wait(barrier, count)
-    start(0, OFFSETS)
 
     for r in range(STEPS - 1):
         t = STEPS - 1 - r

time: 23.8 us -> 23.6 us (level)
  no operation moved by 1% of the time
where the time goes in v5:
time: 23.6 us; the launch traced here: 23.5 us
  Pallas kernels  22.9 us (97%)
  between operations  0.64 us (3%)
    pallas_call x1, Pallas kernels, local(): exchange(saved, porosity, fluid, seed_adjoint.reshape(3, 3, 3, 8, 8, 128))  21.6 us
    pallas_call x1, Pallas kernels, local(): last(*exchange(saved, porosity, fluid, seed_adjoint.reshape(3, 3, 3, 8, 8...  1.31 us

profile of v5, /device:TPU:1, one launch (start us, length us, event | category | flops | bytes accessed | tf_op | source)
XLA Modules:
  0.0 23.5 jit_solution(2865830719544939977)
XLA Ops:
  0.6 21.6 %shard_map.59 = (f32[3,3,3,10,24,128]{5,4,3,2,1,0:T(8,128)S(1)}, f32[2,8,128]{2,1,0:T(8,128)S(1)}, f32[27,8,8,128]{3,2,1,0:T(8,128)S(1)}, f32[4,8,8,128]{3,2,1,0...) custom-call(f32[3,27,8,8,128]{4,3,2,1,0:T(8,128)} %saved.1, ...), custom_call_target="tpu_custom_call" | custom-call | tf_op jit(solution)/shard_map/pallas_call | solution.py:441
  22.2 1.3 %shard_map.60 = (f32[27,8,8,128]{3,2,1,0:T(8,128)}, f32[8,8,128]{2,1,0:T(8,128)}) custom-call(f32[3,3,3,10,24,128]{5,4,3,2,1,0:T(8,128)S(1)} %get-tuple-element.9.adj, f32[2,8,128]{2,1,0:T(8,128)S(1)} %get-tuple-element.10.edges, f32[27,8,8,128]{3,2,1,0:T(8,128)S(1)} %get-tuple-element.11.pops, f32[4,8,8,128]{3,2,1,0:T(8,128)S(1)} %get-tuple-element.12.flow, ...), custom_call_target="tpu_custom_call" | custom-call | tf_op jit(solution)/shard_map/pallas_call | solution.py:441

commit v6 on v5

--- a/solution.py
+++ b/solution.py
@@ -250,31 +250,39 @@
         v = jnp.where(inner == row, jnp.broadcast_to(tile[y : y + 1], (8, 128)), 0.0)
         return [jnp.sum(jnp.where(group == k, v, 0.0), axis=1, keepdims=True) for k in range(9)]
 
-    def outer_plane(r, t, y, sides):
+    def outer_planes(r, t, sides):
         flat = adjs[r].reshape(6480, 128)
         rates = flow[t].reshape(256, 128)
-        there = pl.ds(y, 8, stride=8)
-        p = pull(
-            lambda a, b, c: flat[pl.ds(((9 * a + 3 * b + c) * 10 + a) * 24 + 7 + b + y, 8, stride=24), :],
-            0, [along(side, y) for side in sides], lane,
-        )
-        s = jnp.where(flu.reshape(64, 128)[there, :] == 1, por.reshape(64, 128)[there, :], 1.0)
-        b = 0 if y else 2
-        new = {}
-
-        def store(a, _, c, value):
-            new[a, c] = value
-            plane[r, b // 2, a, c] = value
-
-        new_adjoint(p, terms(p, [rates[pl.ds(64 * k + y, 8, stride=8), :] for k in (1, 2, 3)]), s, store, (b,))
-        for c, edge_lane in ((2, 0), (0, 127)):
-            packed = zero
-            for a in range(3):
-                here = lane == (3 * a + b) * 8 + ((row + 1 - a) & 7)
-                packed = jnp.where(here, jnp.broadcast_to(new[a, c][:, edge_lane : edge_lane + 1], (8, 128)), packed)
-            for n in (4, 2, 1):
-                packed = packed + pltpu.roll(packed, n, 0)
-            zrow[r, b // 2, c // 2] = packed
+        given, made = [], []
+        for y in (0, 7):
+            there = pl.ds(y, 8, stride=8)
+            p = pull(
+                lambda a, b, c: flat[pl.ds(((9 * a + 3 * b + c) * 10 + a) * 24 + 7 + b + y, 8, stride=24), :],
+                0, [along(side, y) for side in sides], lane,
+            )
+            s = jnp.where(flu.reshape(64, 128)[there, :] == 1, por.reshape(64, 128)[there, :], 1.0)
+            given.append((p, [rates[pl.ds(64 * k + y, 8, stride=8), :] for k in (1, 2, 3)], s))
+        for (p, velocity, s), b in zip(given, (2, 0)):
+            new = {}
+            new_adjoint(p, terms(p, velocity), s, lambda a, _, c, value: new.update({(a, c): value}), (b,))
+            rows = []
+            for c, edge_lane in ((2, 0), (0, 127)):
+                packed = zero
+                for a in range(3):
+                    here = lane == (3 * a + b) * 8 + ((row + 1 - a) & 7)
+                    side = jnp.broadcast_to(new[a, c][:, edge_lane : edge_lane + 1], (8, 128))
+                    packed = jnp.where(here, side, packed)
+                for n in (4, 2, 1):
+                    packed = packed + pltpu.roll(packed, n, 0)
+                rows.append((c, packed))
+            made.append((b, new, rows))
+        for b, new, rows in made:
+            for (a, c), value in new.items():
+                plane[r, b // 2, a, c] = value
+        start(r + 1, [off for off in far if not off[2]])
+        for b, new, rows in made:
+            for c, packed in rows:
+                zrow[r, b // 2, c // 2] = packed
 
     def arrive(r):
         made = copies(r)
@@ -356,9 +364,8 @@
         arrive(r)
         sides = edge(r, -1), edge(r, 1)
 
-        outer_plane(r, t, 0, sides)
-        outer_plane(r, t, 7, sides)
-        start(r + 1, far)
+        outer_planes(r, t, sides)
+        start(r + 1, [off for off in far if off[2]])
 
         def step(x, tiles):
             p = pull(slice_of(adjs[r], x), x, sides, lane)

time: 23.6 us -> 23.7 us (level)
  no operation moved by 1% of the time
where the time goes in v6:
time: 23.7 us; the launch traced here: 23.6 us
  Pallas kernels  23 us (97%)
  between operations  0.64 us (3%)
    pallas_call x1, Pallas kernels, local(): exchange(saved, porosity, fluid, seed_adjoint.reshape(3, 3, 3, 8, 8, 128))  21.7 us
    pallas_call x1, Pallas kernels, local(): last(*exchange(saved, porosity, fluid, seed_adjoint.reshape(3, 3, 3, 8, 8...  1.31 us

profile of v6, /device:TPU:1, one launch (start us, length us, event | category | flops | bytes accessed | tf_op | source)
XLA Modules:
  0.0 23.6 jit_solution(3931234515165830709)
XLA Ops:
  0.6 21.7 %shard_map.59 = (f32[3,3,3,10,24,128]{5,4,3,2,1,0:T(8,128)S(1)}, f32[2,8,128]{2,1,0:T(8,128)S(1)}, f32[27,8,8,128]{3,2,1,0:T(8,128)S(1)}, f32[4,8,8,128]{3,2,1,0...) custom-call(f32[3,27,8,8,128]{4,3,2,1,0:T(8,128)} %saved.1, ...), custom_call_target="tpu_custom_call" | custom-call | tf_op jit(solution)/shard_map/pallas_call | solution.py:448
  22.3 1.3 %shard_map.60 = (f32[27,8,8,128]{3,2,1,0:T(8,128)}, f32[8,8,128]{2,1,0:T(8,128)}) custom-call(f32[3,3,3,10,24,128]{5,4,3,2,1,0:T(8,128)S(1)} %get-tuple-element.9.adj, f32[2,8,128]{2,1,0:T(8,128)S(1)} %get-tuple-element.10.edges, f32[27,8,8,128]{3,2,1,0:T(8,128)S(1)} %get-tuple-element.11.pops, f32[4,8,8,128]{3,2,1,0:T(8,128)S(1)} %get-tuple-element.12.flow, ...), custom_call_target="tpu_custom_call" | custom-call | tf_op jit(solution)/shard_map/pallas_call | solution.py:448
